TPU v7x, 512 devices: a whole 4x4x16 slice. The times are simulated.
512 devices in a mesh: dp: 16 (over x, z_hi, core), tm: 8 (over z_lo), height: 4 (over y).
Axes of the slice: x: 4, y: 4, z: 16 (z_hi: 2, z_lo: 8; z = z_hi * 8 + z_lo), core: 2. Of those that a mesh axis runs over, the one named last changes fastest.
Arguments:
- latent: bfloat16 [256, 8, 16, 512], P(('dp', 'tm'), None, None, 'height'), parts along dimension 0, may hold values from -6 to 6
- gain_latent: float32 [512], P('height'), may hold values from 0.25 to 1.75
- shift_latent: float32 [512], P('height'), may hold values from -3 to 3
- conv_latent: bfloat16 [13824, 512], P('tm', 'height'), may hold values from -0.0546875 to 0.0546875
- up_weight: bfloat16 [512, 2048], P('height'), may hold values from -0.25 to 0.25
- gain_block: float32 [256], replicated, may hold values from 0.25 to 1.75
- shift_block: float32 [256], replicated, may hold values from -3 to 3
- conv_block: bfloat16 [6912, 256], P(('tm', 'height')), may hold values from -0.078125 to 0.078125
- cotangent: bfloat16 [512, 16, 32, 256], P(('dp', 'tm'), 'height'), parts along dimension 0, may hold values from -6 to 6
Outputs:
- decoded: bfloat16 [512, 16, 32, 256], P(('dp', 'tm'), 'height'), parts along dimension 0
- grad_upsampled: bfloat16 [512, 16, 32, 256], P(('dp', 'tm'), 'height'), parts along dimension 0
- grad_weight: float32 [36864, 256], P(('dp', 'tm', 'height')), parts along dimension 0
- grad_gain: float32 [4096], P('dp'), parts along dimension 0
- grad_shift: float32 [4096], P('dp'), parts along dimension 0
There are 16 independent parts, one for each index of `dp`. A program takes and returns all parts, laid end to end along the dimension named above; an argument that names none is the same for every part. Nothing has to cross between parts.
All inputs are finite; a program needn't handle non-finite values.
Results may differ from a plain program's by a relative error of at most 0.009.
Values may be sent and summed in bfloat16 or wider, within the bound.
No kernel may reach another device: no remote copies, remote signals or barrier semaphores. Data moves between devices by JAX's collectives and lax.ppermute only.
A program may use at most 128 MiB of HBM per device.

v0:
```python
import jax
import jax.numpy as jnp
from jax import lax
from jax.sharding import PartitionSpec as P

C1 = 512
GROUPS = 32
epsilon = 1e-06


def copy_for_each(array, axis):
    devices = lax.axis_size(axis)
    return lax.all_to_all(
        jnp.broadcast_to(array[None], (devices, *array.shape)), axis, 0, 0, tiled=True
    )


def taken_together(array, axis):
    everything = copy_for_each(array, axis)
    return jnp.sum(everything, axis=0)


def packed_total(arrays, axis):
    ends = [0]
    for a in arrays:
        ends.append(ends[-1] + a.size)
    so_far = taken_together(jnp.concatenate([a.ravel() for a in arrays]), axis)
    return tuple((so_far[b:e].reshape(a.shape) for a, b, e in zip(arrays, ends, ends[1:])))


def shifted(block, axis, distance):
    devices = range(lax.axis_size(axis))
    route = [(i - distance, i) for i in devices if i - distance in devices]
    return lax.ppermute(block, axis, route)


def in_order(tiles, dim):
    tiles = jnp.moveaxis(tiles, 0, dim)
    shape = tiles.shape
    return tiles.reshape(*shape[:dim], shape[dim] * shape[dim + 1], *shape[dim + 2 :])


def gather_directly(array, axis, dim):
    tiles = copy_for_each(array, axis)
    return in_order(tiles, dim)


def extended_2(cells, sides, width):
    for axis, dim in sides:
        count = lax.axis_size(axis)
        ends = count - 1
        head = lax.slice_in_dim(cells, 0, width, axis=dim)
        tail = lax.slice_in_dim(cells, cells.shape[dim] - width, cells.shape[dim], axis=dim)
        cells = jnp.concatenate(
            [
                lax.ppermute(tail, axis, [(i, (i + 1) % count) for i in range(ends)]),
                cells,
                lax.ppermute(head, axis, [((i + 1) % count, i) for i in range(ends)]),
            ],
            axis=dim,
        )
    return cells


def gather_in_order(array, axes, turns):
    tiles = array
    for k in turns:
        tiles = lax.all_gather(tiles, axes[k])
    done = turns[::-1]
    back = [done.index(k) for k in range(len(axes))]
    tiles = tiles.transpose(*back, *range(len(axes), tiles.ndim))
    return tiles.reshape(-1, *array.shape)


def whole_of(array, axes, turns, dim):
    return in_order(gather_in_order(array, axes, turns), dim)


def cut_along(array, dim, devices):
    before, after = (array.shape[:dim], array.shape[dim + 1 :])
    return jnp.moveaxis(array.reshape(*before, devices, -1, *after), dim, 0)


def sum_at_owner(array, axis, dim):
    tiles = cut_along(array, dim, lax.axis_size(axis))
    arrived = lax.all_to_all(tiles, axis, split_axis=0, concat_axis=0, tiled=True)
    return arrived.sum(axis=0)


def standardize(values, mean_value, inverse, groups):
    shape_full = values.shape
    grouped = values.reshape(shape_full[:-1] + (groups, shape_full[-1] // groups))
    return ((grouped - mean_value[:, None]) * inverse[:, None]).reshape(shape_full)


def causal_taps(padded, weight, frames, rows, cols):
    channels_in = padded.shape[-1]
    summed = jnp.zeros((frames * rows * cols, weight.shape[1]), jnp.float32)
    for lag_step in range(3):
        for row_step in range(3):
            for col_step in range(3):
                tap_index = (lag_step * 3 + row_step) * 3 + col_step
                window = padded[
                    lag_step : lag_step + frames,
                    row_step : row_step + rows,
                    col_step : col_step + cols,
                ]
                kernel = weight[tap_index * channels_in : (tap_index + 1) * channels_in]
                summed = summed + jnp.dot(
                    window.reshape(-1, channels_in), kernel, preferred_element_type=jnp.float32
                )
    return summed.reshape(frames, rows, cols, weight.shape[1])


def transposed_taps(padded, weight, frames, rows, cols):
    channels_out = padded.shape[-1]
    channels_in = weight.shape[0] // 27
    summed = jnp.zeros((frames * rows * cols, channels_in), jnp.float32)
    for lag_step in range(3):
        for row_step in range(3):
            for col_step in range(3):
                tap_index = (lag_step * 3 + row_step) * 3 + col_step
                window = padded[
                    2 - lag_step : 2 - lag_step + frames,
                    2 - row_step : 2 - row_step + rows,
                    2 - col_step : 2 - col_step + cols,
                ]
                kernel = weight[tap_index * channels_in : (tap_index + 1) * channels_in]
                summed = summed + lax.dot_general(
                    window.reshape(-1, channels_out),
                    kernel,
                    (((1,), (1,)), ((), ())),
                    preferred_element_type=jnp.float32,
                )
    return summed.reshape(frames, rows, cols, channels_in)


def weight_terms(padded, grads, frames, rows, cols):
    channels_in = padded.shape[-1]
    flat_grads = grads.reshape(-1, grads.shape[-1])
    blocks = []
    for row_step in range(3):
        for col_step in range(3):
            window = padded[2 : 2 + frames, row_step : row_step + rows, col_step : col_step + cols]
            blocks.append(
                lax.dot_general(
                    window.reshape(-1, channels_in),
                    flat_grads,
                    (((0,), (0,)), ((), ())),
                    preferred_element_type=jnp.float32,
                )
            )
    return jnp.concatenate(blocks, 0)


def local(
    latent,
    gain_latent,
    shift_latent,
    conv_latent,
    up_weight,
    gain_block,
    shift_block,
    conv_block,
    cotangent,
):
    per_group = C1 // GROUPS
    groups_here = latent.shape[-1] // per_group
    latent_f32 = latent.astype(jnp.float32)
    grouped = latent_f32.reshape(-1, groups_here, per_group)
    first_sums = jnp.sum(grouped, axis=(0, 2))
    second_sums = jnp.sum(grouped * grouped, axis=(0, 2))
    first_totals, second_totals = packed_total((first_sums, second_sums), "tm")
    count_latent = grouped.shape[0] * per_group * lax.axis_size("tm")
    mean_latent = first_totals / count_latent
    inverse_latent = lax.rsqrt(second_totals / count_latent - mean_latent * mean_latent + epsilon)
    normed = (
        standardize(latent_f32, mean_latent, inverse_latent, groups_here) * gain_latent
        + shift_latent
    )
    active = jax.nn.silu(normed).astype(jnp.bfloat16)
    earlier = shifted(active, "tm", 1)
    extended = jnp.concatenate([earlier, active], 0)
    all_channels = gather_directly(extended, "height", 3)
    padded = jnp.pad(all_channels, ((0, 0), (1, 1), (1, 1), (0, 0)))
    latent_weight = lax.all_gather(conv_latent, "tm", axis=0, tiled=True)
    frames_latent, rows_latent, cols_latent = (latent.shape[0], latent.shape[1], latent.shape[2])
    mixed = causal_taps(padded, latent_weight, frames_latent, rows_latent, cols_latent)
    refined = (latent_f32 + mixed).astype(jnp.bfloat16)
    band_rows = rows_latent // lax.axis_size("height")
    own_band = lax.all_to_all(refined, "height", split_axis=1, concat_axis=3, tiled=True)
    flat_band = own_band.reshape(-1, own_band.shape[-1])
    expanded = jnp.dot(
        flat_band, gather_directly(up_weight, "height", 0), preferred_element_type=jnp.float32
    )
    channels_block = up_weight.shape[1] // 8
    spread = expanded.reshape(frames_latent, band_rows, cols_latent, 2, 2, 2, channels_block)
    spread = spread.transpose(0, 3, 1, 4, 2, 5, 6)
    upsampled = spread.reshape(
        2 * frames_latent, 2 * band_rows, 2 * cols_latent, channels_block
    ).astype(jnp.bfloat16)
    frames_block, rows_block, cols_block = (
        upsampled.shape[0],
        upsampled.shape[1],
        upsampled.shape[2],
    )
    up_f32 = upsampled.astype(jnp.float32)
    per_block = channels_block // GROUPS
    grouped_block = up_f32.reshape(-1, GROUPS, per_block)
    block_first = jnp.sum(grouped_block, axis=(0, 2))
    block_second = jnp.sum(grouped_block * grouped_block, axis=(0, 2))
    block_first, block_second = packed_total((block_first, block_second), ("tm", "height"))
    count_block = grouped_block.shape[0] * per_block * lax.axis_size("tm") * lax.axis_size("height")
    mean_block = block_first / count_block
    inverse_block = lax.rsqrt(block_second / count_block - mean_block * mean_block + epsilon)
    standard = standardize(up_f32, mean_block, inverse_block, GROUPS)
    normed_block = standard * gain_block + shift_block
    active_block = jax.nn.silu(normed_block).astype(jnp.bfloat16)
    before = shifted(active_block[-2:], "tm", 1)
    ext_block = jnp.concatenate([before, active_block], 0)
    beside_all = extended_2(ext_block, (("height", 1),), 1)
    padded_block = jnp.pad(beside_all, ((0, 0), (0, 0), (1, 1), (0, 0)))
    block_weight = whole_of(conv_block, ("tm", "height"), (0, 1), 0)
    mixed_block = causal_taps(padded_block, block_weight, frames_block, rows_block, cols_block)
    decoded = (up_f32 + mixed_block).astype(jnp.bfloat16)
    after = shifted(cotangent[:2], "tm", -1)
    grad_ext = jnp.concatenate([cotangent, after], 0)
    grad_around = extended_2(grad_ext, (("height", 1),), 1)
    grad_padded = jnp.pad(grad_around, ((0, 0), (0, 0), (1, 1), (0, 0)))
    grad_active = transposed_taps(grad_padded, block_weight, frames_block, rows_block, cols_block)
    local_terms = weight_terms(padded_block, cotangent, frames_block, rows_block, cols_block)
    time_summed = sum_at_owner(local_terms, "tm", 0)
    grad_weight = sum_at_owner(time_summed, "height", 0)
    sigmoid = jax.nn.sigmoid(normed_block)
    grad_normed = grad_active * sigmoid * (1.0 + normed_block * (1.0 - sigmoid))
    flat_grad = grad_normed.reshape(-1, channels_block)
    flat_standard = standard.reshape(-1, channels_block)
    grad_shift, grad_gain = packed_total(
        (jnp.sum(flat_grad, axis=0), jnp.sum(flat_grad * flat_standard, axis=0)), ("tm", "height")
    )
    first_mean = jnp.sum((gain_block * grad_shift).reshape(GROUPS, per_block), axis=1) / count_block
    second_mean = jnp.sum((gain_block * grad_gain).reshape(GROUPS, per_block), axis=1) / count_block
    grouped_grad = (grad_normed * gain_block).reshape(-1, GROUPS, per_block)
    grouped_standard = standard.reshape(-1, GROUPS, per_block)
    corrected = (
        grouped_grad - first_mean[:, None] - grouped_standard * second_mean[:, None]
    ) * inverse_block[:, None]
    grad_upsampled = (cotangent.astype(jnp.float32) + corrected.reshape(cotangent.shape)).astype(
        jnp.bfloat16
    )
    return (decoded, grad_upsampled, grad_weight, grad_gain, grad_shift)


def solution(mesh):
    return jax.shard_map(
        local,
        mesh=mesh,
        in_specs=(
            P(("dp", "tm"), None, None, "height"),
            P("height"),
            P("height"),
            P("tm", "height"),
            P("height", None),
            P(),
            P(),
            P(("tm", "height"), None),
            P(("dp", "tm"), "height", None, None),
        ),
        out_specs=(
            P(("dp", "tm"), "height", None, None),
            P(("dp", "tm"), "height", None, None),
            P(("dp", "tm", "height"), None),
            P("dp"),
            P("dp"),
        ),
        check_vma=False,
    )
```

profile of v0, /device:TPU:2, one launch (start us, length us, event | category | flops | bytes accessed | tf_op | source)
XLA Modules:
  0.0 456.5 jit_solution(3244054950084139941)
XLA Ops:
  7.2 54.2 %all-gather = bf16[1728,256]{1,0:T(8,128)(2,1)} all-gather(bf16[216,256]{1,0:T(8,128)(2,1)} %param.16), channel_id=2, replica_groups=mesh['dp'=16,'tm'=8,'height'=4] {'tm'}, dimensions={0}, use_global_device_ids=true | all-gather | bytes 995328 | tf_op jit(solution)/shard_map/all_gather | solution.py:68
  63.4 10.3 %all-to-all-start = ((f32[8,1,16]{2,1,0:T(1,128)}), f32[8,1,16]{2,1,0:T(1,128)S(1)}, u32[]{:S(2)}, u32[]{:S(2)}) async-start(f32[8,1,16]{2,1,0:T(1,128)} %broadcast_in_dim.10), calls=%async_computation | async-start | bytes 8192 | tf_op jit(solution)/shard_map/all_to_all | solution.py:13
  73.7 0.9 slice.629
  74.6 1.3 collective-permute-start.4
  75.9 8.1 %all-to-all-done = f32[8,1,16]{2,1,0:T(1,128)S(1)} async-done(((f32[8,1,16]{2,1,0:T(1,128)}), f32[8,1,16]{2,1,0:T(1,128)S(1)}, u32[]{:S(2)}, u32[]{:S(2)}) %all-to-all-start) | async-done | bytes 544 | tf_op jit(solution)/shard_map/all_to_all | solution.py:13
  84.4 0.9 fusion.44
  85.3 2.5 collective-permute-start
  87.8 1.0 constant_dynamic-update-slice_fusion.1
  88.8 0.9 collective-permute-done
  89.8 0.9 broadcast_in_dim.11
  90.7 4.5 all-to-all-start.1
  95.2 1.3 collective-permute-start.6
  96.5 4.6 collective-permute-start.5
  101.4 8.3 %all-to-all-done.1 = bf16[4,4,8,16,128]{4,3,2,1,0:T(8,128)(2,1)S(1)} async-done(((bf16[4,4,8,16,128]{4,3,2,1,0:T(8,128)(2,1)}), bf16[4,4,8,16,128]{4,3,2,1,0:T(8,128)(2,1)S(1)}, u32[]{:S(2)}, u32[]{:S(2)}) %all-to-all-start.1) | async-done | bytes 524320 | tf_op jit(solution)/shard_map/all_to_all | solution.py:13
  109.6 1.7 broadcast_in_dim.12
  111.3 3.6 all-to-all-start.3
  115.3 1.4 pad_maximum_fusion.1
  116.7 2.2 fusion.149
  119.1 0.9 copy.69
  121.9 1.2 pad_slice_fusion.1
  123.1 2.4 pad_slice_fusion
  125.4 19.1 %all-to-all-done.3 = bf16[4,128,2048]{1,2,0:T(8,128)(2,1)S(1)} async-done(((bf16[4,128,2048]{1,2,0:T(8,128)(2,1)}), bf16[4,128,2048]{1,2,0:T(8,128)(2,1)S(1)}, u32[]{:S(2)}, u32[]{:S(2)}) %all-to-all-start.3) | async-done | bytes 2097184 | tf_op jit(solution)/shard_map/all_to_all | solution.py:13
  144.5 2.6 copy.75
  147.2 3.9 copy.76
  151.1 2.4 copy.79
  160.1 1.1 convolution_add_fusion.2
  161.2 68.7 %all-gather.5.cloned.1.call-done = bf16[13824,128]{1,0:T(8,128)(2,1)} async-done(((bf16[1728,128]{1,0:T(8,128)(2,1)}), bf16[13824,128]{1,0:T(8,128)(2,1)}) %all-gather.5.cloned.1.call-update) | async-done | bytes 3538960 | tf_op jit(solution)/shard_map/all_gather | solution.py:186
  229.9 1.3 fusion.72
  231.3 1.4 convolution_add_fusion.72
  232.6 1.2 convolution_add_fusion.71
  233.9 1.2 convolution_add_fusion.70
  235.1 1.2 convolution_add_fusion.69
  236.4 1.2 convolution_add_fusion.68
  237.7 1.2 convolution_add_fusion.67
  238.9 1.2 convolution_add_fusion.66
  245.2 4.2 all-to-all-start.2
  249.4 2.2 convolution_add_fusion.1
  251.6 3.6 all-to-all-done.2
  255.2 1.5 copy.119
  256.7 1.5 reshape.488
  258.2 3.7 fusion.146
  266.1 4.8 %all-to-all-start.4 = ((f32[32,1,64]{2,1,0:T(1,128)}), f32[32,1,64]{2,1,0:T(1,128)S(1)}, u32[]{:S(2)}, u32[]{:S(2)}) async-start(f32[32,1,64]{2,1,0:T(1,128)} %broadcast_in_dim.13), calls=%async_computation.4 | async-start | bytes 32768 | tf_op jit(solution)/shard_map/all_to_all | solution.py:13
  270.9 2.0 fusion.74
  272.9 2.2 copy.77
  275.2 2.2 reshape.485
  277.4 5.9 %all-to-all-done.4 = f32[32,1,64]{2,1,0:T(1,128)S(1)} async-done(((f32[32,1,64]{2,1,0:T(1,128)}), f32[32,1,64]{2,1,0:T(1,128)S(1)}, u32[]{:S(2)}, u32[]{:S(2)}) %all-to-all-start.4) | async-done | bytes 8224 | tf_op jit(solution)/shard_map/all_to_all | solution.py:13
  283.8 1.2 slice_multiply_fusion
  287.1 2.8 fusion.145
  290.6 6.5 %all-to-all-start.5 = ((f32[32,1,512]{2,1,0:T(1,128)}), f32[32,1,512]{2,1,0:T(1,128)S(1)}, u32[]{:S(2)}, u32[]{:S(2)}) async-start(f32[32,1,512]{2,1,0:T(1,128)} %broadcast_in_dim.14), calls=%async_computation.5 | async-start | bytes 131072 | tf_op jit(solution)/shard_map/all_to_all | solution.py:13
  297.1 1.4 reshape.484
  298.5 11.5 %all-to-all-done.5 = f32[32,1,512]{2,1,0:T(1,128)S(1)} async-done(((f32[32,1,512]{2,1,0:T(1,128)}), f32[32,1,512]{2,1,0:T(1,128)S(1)}, u32[]{:S(2)}, u32[]{:S(2)}) %all-to-all-start.5) | async-done | bytes 65568 | tf_op jit(solution)/shard_map/all_to_all | solution.py:13
  311.4 2.2 add_convert_fusion
  313.6 2.3 collective-permute-start.1
  315.9 2.5 collective-permute-done.1
  318.5 1.3 collective-permute-start.3
  319.8 4.6 collective-permute-start.2
  325.0 1.5 collective-permute-done.2
  329.4 1.4 copy-done.9
  330.8 5.2 %all-to-all-start.6 = ((f32[8,288,256]{2,1,0:T(8,128)}), f32[8,288,256]{2,1,0:T(8,128)S(1)}, u32[]{:S(2)}, u32[]{:S(2)}) async-start(f32[8,288,256]{2,1,0:T(8,128)} %bitcast.329), calls=%async_computation.6 | async-start | bytes 4718592 | tf_op jit(solution)/shard_map/all_to_all | solution.py:86
  336.1 1.0 pad_maximum_fusion
  337.9 1.3 copy-done.1
  345.7 91.6 %all-to-all-done.6 = f32[8,288,256]{2,1,0:T(8,128)S(1)} async-done(((f32[8,288,256]{2,1,0:T(8,128)}), f32[8,288,256]{2,1,0:T(8,128)S(1)}, u32[]{:S(2)}, u32[]{:S(2)}) %all-to-all-start.6) | async-done | bytes 2359328 | tf_op jit(solution)/shard_map/all_to_all | solution.py:86
  438.2 4.0 all-to-all-start.7
  443.0 6.1 %all-to-all-done.7 = f32[4,72,256]{2,1,0:T(8,128)S(1)} async-done(((f32[4,72,256]{2,1,0:T(8,128)}), f32[4,72,256]{2,1,0:T(8,128)S(1)}, u32[]{:S(2)}, u32[]{:S(2)}) %all-to-all-start.7) | async-done | bytes 294944 | tf_op jit(solution)/shard_map/all_to_all | solution.py:86
  (265 shorter events, 38.0 us)
Async XLA Ops:
  7.2 93.9 %copy-start.53 = (bf16[128,2048]{1,0:T(8,128)(2,1)S(1)}, bf16[128,2048]{1,0:T(8,128)(2,1)}, u32[]{:S(2)}) copy-start(bf16[128,2048]{1,0:T(8,128)(2,1)} %param.13) | copy-start | bytes 1572868
  7.2 143.9 %all-gather.7.cloned.1.call-start = ((), (), s32[]{:S(2)}) async-start(), calls=%async_computation.9 | async-start | bytes 4423680 | tf_op jit(solution)/shard_map/all_gather | solution.py:68
  63.4 20.6 %all-to-all-start = ((f32[8,1,16]{2,1,0:T(1,128)}), f32[8,1,16]{2,1,0:T(1,128)S(1)}, u32[]{:S(2)}, u32[]{:S(2)}) async-start(f32[8,1,16]{2,1,0:T(1,128)} %broadcast_in_dim.10), calls=%async_computation | async-start | bytes 8192 | tf_op jit(solution)/shard_map/all_to_all | solution.py:13
  74.6 20.5 %collective-permute-start.4 = (bf16[2,4,32,256]{3,2,1,0:T(8,128)(2,1)S(1)}, bf16[2,4,32,256]{3,2,1,0:T(8,128)(2,1)S(1)}, u32[]{:S(2)}, u32[]{:S(2)}) collective-permute-start(bf16[2,4,32,256]{3,2,1,0:T(8,128)(2,1)S(1)} %slice.629), channel_id=1, source_target_pairs={{4,0},{8,4},{12,8},{16,12},{20,16},{24,20},{28,24},{5,1},{9,5},{13... | collective-permute-start | bytes 393224 | tf_op jit(solution)/shard_map/ppermute | solution.py:34
  85.3 4.4 collective-permute-start
  90.7 18.9 %all-to-all-start.1 = ((bf16[4,4,8,16,128]{4,3,2,1,0:T(8,128)(2,1)}), bf16[4,4,8,16,128]{4,3,2,1,0:T(8,128)(2,1)S(1)}, u32[]{:S(2)}, u32[]{:S(2)}) async-start(bf16[4,4,8,16,128]{4,3,2,1,0:T(8,128)(2,1)} %broadcast_in_dim.11), calls=%async_computation.1 | async-start | bytes 1048576 | tf_op jit(solution)/shard_map/all_to_all | solution.py:13
  95.1 134.7 %all-gather.5.cloned.1.call-start = ((), (), s32[]{:S(2)}) async-start(), calls=%async_computation.8 | async-start | bytes 3981312 | tf_op jit(solution)/shard_map/all_gather | solution.py:186
  95.2 19.7 %collective-permute-start.6 = (bf16[6,1,32,256]{3,2,1,0:T(8,128)(2,1)S(1)}, bf16[6,1,32,256]{3,2,1,0:T(8,128)(2,1)S(1)}, u32[]{:S(2)}, u32[]{:S(2)}) collective-permute-start(bf16[6,1,32,256]{3,2,1,0:T(8,128)(2,1)S(1)} %get-tuple-element.98), channel_id=1, source_target_pairs={{1,0},{2,1},{3,2},{5,4},{6,5},{7,6},{9,8},{10,9},{11,10},{13,12},{... | collective-permute-start | bytes 294920 | tf_op jit(solution)/shard_map/ppermute | solution.py:58
  96.5 18.4 %collective-permute-start.5 = (bf16[6,1,32,256]{3,2,1,0:T(8,128)(2,1)S(1)}, bf16[6,1,32,256]{3,2,1,0:T(8,128)(2,1)S(1)}, u32[]{:S(2)}, u32[]{:S(2)}) collective-permute-start(bf16[6,1,32,256]{3,2,1,0:T(8,128)(2,1)S(1)} %get-tuple-element.97), channel_id=1, source_target_pairs={{0,1},{1,2},{2,3},{4,5},{5,6},{6,7},{8,9},{9,10},{10,11},{12,13},{... | collective-permute-start | bytes 294920 | tf_op jit(solution)/shard_map/ppermute | solution.py:56
  109.6 1.7 copy-start.2
  111.3 33.2 %all-to-all-start.3 = ((bf16[4,128,2048]{1,2,0:T(8,128)(2,1)}), bf16[4,128,2048]{1,2,0:T(8,128)(2,1)S(1)}, u32[]{:S(2)}, u32[]{:S(2)}) async-start(bf16[4,128,2048]{1,2,0:T(8,128)(2,1)} %broadcast_in_dim.12), calls=%async_computation.3 | async-start | bytes 4194304 | tf_op jit(solution)/shard_map/all_to_all | solution.py:13
  116.7 2.2 copy-start.3
  151.1 2.4 copy-start.16
  151.1 2.7 copy-start.15
  151.1 3.0 copy-start.14
  151.1 3.3 copy-start.13
  153.5 133.6 %copy-start = (bf16[8,4,216,256]{3,2,1,0:T(8,128)(2,1)}, bf16[8,4,216,256]{3,2,1,0:T(8,128)(2,1)S(1)}, u32[]{:S(2)}) copy-start(bf16[8,4,216,256]{3,2,1,0:T(8,128)(2,1)S(1)} %copy.79) | copy-start | bytes 10616836
  153.5 1.7 copy-start.37
  153.8 1.7 copy-start.12
  154.4 1.5 copy-start.36
  154.7 1.4 copy-start.30
  155.0 1.4 copy-start.35
  155.3 1.4 copy-start.33
  157.0 1.4 copy-start.23
  157.3 1.4 copy-start.28
  157.5 1.4 copy-start.27
  229.9 7.8 %copy-start.6 = (bf16[13824,128]{1,0:T(8,128)(2,1)S(1)}, bf16[13824,128]{1,0:T(8,128)(2,1)}, u32[]{:S(2)}) copy-start(bf16[13824,128]{1,0:T(8,128)(2,1)} %all-gather.5.cloned.1.call-done) | copy-start | bytes 10616836
  229.9 10.2 %copy-start.51 = (bf16[2,8,16,512]{3,2,1,0:T(8,128)(2,1)S(1)}, bf16[2,8,16,512]{3,2,1,0:T(8,128)(2,1)}, u32[]{:S(2)}) copy-start(bf16[2,8,16,512]{3,2,1,0:T(8,128)(2,1)} %get-tuple-element.60) | copy-start | bytes 786436
  229.9 10.4 %copy-start.50 = (bf16[2,8,16,512]{3,2,1,0:T(8,128)(2,1)S(1)}, bf16[2,8,16,512]{3,2,1,0:T(8,128)(2,1)}, u32[]{:S(2)}) copy-start(bf16[2,8,16,512]{3,2,1,0:T(8,128)(2,1)} %get-tuple-element.61) | copy-start | bytes 786436
  229.9 10.7 %copy-start.49 = (bf16[2,8,16,512]{3,2,1,0:T(8,128)(2,1)S(1)}, bf16[2,8,16,512]{3,2,1,0:T(8,128)(2,1)}, u32[]{:S(2)}) copy-start(bf16[2,8,16,512]{3,2,1,0:T(8,128)(2,1)} %get-tuple-element.62) | copy-start | bytes 786436
  229.9 10.9 %copy-start.48 = (bf16[2,8,16,512]{3,2,1,0:T(8,128)(2,1)S(1)}, bf16[2,8,16,512]{3,2,1,0:T(8,128)(2,1)}, u32[]{:S(2)}) copy-start(bf16[2,8,16,512]{3,2,1,0:T(8,128)(2,1)} %get-tuple-element.63) | copy-start | bytes 786436
  231.2 9.8 %copy-start.47 = (bf16[2,8,16,512]{3,2,1,0:T(8,128)(2,1)S(1)}, bf16[2,8,16,512]{3,2,1,0:T(8,128)(2,1)}, u32[]{:S(2)}) copy-start(bf16[2,8,16,512]{3,2,1,0:T(8,128)(2,1)} %get-tuple-element.64) | copy-start | bytes 786436
  232.6 8.7 %copy-start.22 = (bf16[2,8,16,4,128]{4,3,2,1,0:T(4,128)(2,1)S(1)}, bf16[2,8,16,4,128]{4,3,2,1,0:T(4,128)(2,1)}, u32[]{:S(2)}) copy-start(bf16[2,8,16,4,128]{4,3,2,1,0:T(4,128)(2,1)} %copy.70) | copy-start | bytes 786436
  233.9 7.7 %copy-start.46 = (bf16[2,8,16,512]{3,2,1,0:T(8,128)(2,1)S(1)}, bf16[2,8,16,512]{3,2,1,0:T(8,128)(2,1)}, u32[]{:S(2)}) copy-start(bf16[2,8,16,512]{3,2,1,0:T(8,128)(2,1)} %get-tuple-element.65) | copy-start | bytes 786436
  235.1 6.6 %copy-start.45 = (bf16[2,8,16,512]{3,2,1,0:T(8,128)(2,1)S(1)}, bf16[2,8,16,512]{3,2,1,0:T(8,128)(2,1)}, u32[]{:S(2)}) copy-start(bf16[2,8,16,512]{3,2,1,0:T(8,128)(2,1)} %get-tuple-element.66) | copy-start | bytes 786436
  236.4 5.6 %copy-start.44 = (bf16[2,8,16,512]{3,2,1,0:T(8,128)(2,1)S(1)}, bf16[2,8,16,512]{3,2,1,0:T(8,128)(2,1)}, u32[]{:S(2)}) copy-start(bf16[2,8,16,512]{3,2,1,0:T(8,128)(2,1)} %get-tuple-element.67) | copy-start | bytes 786436
  237.6 4.6 %copy-start.43 = (bf16[2,8,16,512]{3,2,1,0:T(8,128)(2,1)S(1)}, bf16[2,8,16,512]{3,2,1,0:T(8,128)(2,1)}, u32[]{:S(2)}) copy-start(bf16[2,8,16,512]{3,2,1,0:T(8,128)(2,1)} %get-tuple-element.68) | copy-start | bytes 786436
  238.9 3.6 copy-start.42
  240.1 2.6 copy-start.41
  240.3 2.6 copy-start.40
  240.6 2.6 copy-start.20
  240.8 2.6 copy-start.21
  241.1 2.6 copy-start.19
  241.3 2.6 copy-start.18
  241.5 2.5 copy-start.17
  241.8 2.5 copy-start.39
  242.0 2.5 copy-start.52
  245.2 10.0 %all-to-all-start.2 = ((bf16[2,8,16,128]{3,2,0,1:T(8,128)(2,1)}), bf16[2,8,16,128]{3,2,0,1:T(8,128)(2,1)}, u32[]{:S(2)}, u32[]{:S(2)}) async-start(bf16[2,8,16,128]{3,2,0,1:T(8,128)(2,1)} %fusion.45), calls=%async_computation.2 | async-start | bytes 131072 | tf_op jit(solution)/shard_map/all_to_all | solution.py:191
  266.1 17.1 %all-to-all-start.4 = ((f32[32,1,64]{2,1,0:T(1,128)}), f32[32,1,64]{2,1,0:T(1,128)S(1)}, u32[]{:S(2)}, u32[]{:S(2)}) async-start(f32[32,1,64]{2,1,0:T(1,128)} %broadcast_in_dim.13), calls=%async_computation.4 | async-start | bytes 32768 | tf_op jit(solution)/shard_map/all_to_all | solution.py:13
  287.1 22.9 %copy-start.57 = (f32[256]{0:T(256)S(1)}, f32[256]{0:T(256)}, u32[]{:S(2)}) copy-start(f32[256]{0:T(256)} %param.14) | copy-start | bytes 3076
  287.1 24.3 %copy-start.58 = (f32[256]{0:T(256)S(1)}, f32[256]{0:T(256)}, u32[]{:S(2)}) copy-start(f32[256]{0:T(256)} %mul.160) | copy-start | bytes 3076
  287.1 24.3 %copy-start.59 = (f32[256]{0:T(256)S(1)}, f32[256]{0:T(256)}, u32[]{:S(2)}) copy-start(f32[256]{0:T(256)} %sub.74) | copy-start | bytes 3076
  287.1 24.3 %copy-start.60 = (f32[256]{0:T(256)S(1)}, f32[256]{0:T(256)}, u32[]{:S(2)}) copy-start(f32[256]{0:T(256)} %param.15) | copy-start | bytes 3076
  289.9 37.0 %copy-start.8 = (bf16[4,4,32,256]{3,2,1,0:T(8,128)(2,1)S(1)}, bf16[4,4,32,256]{3,2,1,0:T(8,128)(2,1)}, u32[]{:S(2)}) copy-start(bf16[4,4,32,256]{3,2,1,0:T(8,128)(2,1)} %param.17) | copy-start | bytes 786436
  290.6 19.4 %all-to-all-start.5 = ((f32[32,1,512]{2,1,0:T(1,128)}), f32[32,1,512]{2,1,0:T(1,128)S(1)}, u32[]{:S(2)}, u32[]{:S(2)}) async-start(f32[32,1,512]{2,1,0:T(1,128)} %broadcast_in_dim.14), calls=%async_computation.5 | async-start | bytes 131072 | tf_op jit(solution)/shard_map/all_to_all | solution.py:13
  298.5 26.5 %copy-start.4 = (f32[4,4,32,256]{3,2,1,0:T(8,128)}, f32[4,4,32,256]{3,2,1,0:T(8,128)S(1)}, u32[]{:S(2)}) copy-start(f32[4,4,32,256]{3,2,1,0:T(8,128)S(1)} %reshape.484) | copy-start | bytes 1572868
  313.6 4.8 %collective-permute-start.1 = (bf16[2,4,32,256]{3,2,1,0:T(8,128)(2,1)S(1)}, bf16[2,4,32,256]{3,2,1,0:T(8,128)(2,1)S(1)}, u32[]{:S(2)}, u32[]{:S(2)}) collective-permute-start(bf16[2,4,32,256]{3,2,1,0:T(8,128)(2,1)S(1)} %slice.690), channel_id=1, source_target_pairs={{0,4},{4,8},{8,12},{12,16},{16,20},{20,24},{24,28},{1,5},{5,9},{9,... | collective-permute-start | bytes 393224 | tf_op jit(solution)/shard_map/ppermute | solution.py:34
  318.5 6.5 %collective-permute-start.3 = (bf16[6,1,32,256]{3,2,1,0:T(8,128)(2,1)S(1)}, bf16[6,1,32,256]{3,2,1,0:T(8,128)(2,1)S(1)}, u32[]{:S(2)}, u32[]{:S(2)}) collective-permute-start(bf16[6,1,32,256]{3,2,1,0:T(8,128)(2,1)S(1)} %get-tuple-element.104), channel_id=1, source_target_pairs={{1,0},{2,1},{3,2},{5,4},{6,5},{7,6},{9,8},{10,9},{11,10},{13,12},{... | collective-permute-start | bytes 294920 | tf_op jit(solution)/shard_map/ppermute | solution.py:58
  319.8 6.8 %collective-permute-start.2 = (bf16[6,1,32,256]{3,2,1,0:T(8,128)(2,1)S(1)}, bf16[6,1,32,256]{3,2,1,0:T(8,128)(2,1)S(1)}, u32[]{:S(2)}, u32[]{:S(2)}) collective-permute-start(bf16[6,1,32,256]{3,2,1,0:T(8,128)(2,1)S(1)} %get-tuple-element.103), channel_id=1, source_target_pairs={{0,1},{1,2},{2,3},{4,5},{5,6},{6,7},{8,9},{9,10},{10,11},{12,13},{... | collective-permute-start | bytes 294920 | tf_op jit(solution)/shard_map/ppermute | solution.py:56
  325.0 3.9 copy-start.55
  330.8 106.5 %all-to-all-start.6 = ((f32[8,288,256]{2,1,0:T(8,128)}), f32[8,288,256]{2,1,0:T(8,128)S(1)}, u32[]{:S(2)}, u32[]{:S(2)}) async-start(f32[8,288,256]{2,1,0:T(8,128)} %bitcast.329), calls=%async_computation.6 | async-start | bytes 4718592 | tf_op jit(solution)/shard_map/all_to_all | solution.py:86
  337.1 2.0 copy-start.1
  345.0 97.2 %copy-start.5 = (f32[4,4,32,256]{3,2,1,0:T(8,128)S(1)}, f32[4,4,32,256]{3,2,1,0:T(8,128)}, u32[]{:S(2)}) copy-start(f32[4,4,32,256]{3,2,1,0:T(8,128)} %copy-done.4) | copy-start | bytes 1572868
  438.2 10.8 %all-to-all-start.7 = ((f32[4,72,256]{2,1,0:T(8,128)}), f32[4,72,256]{2,1,0:T(8,128)S(1)}, u32[]{:S(2)}, u32[]{:S(2)}) async-start(f32[4,72,256]{2,1,0:T(8,128)} %bitcast.332), calls=%async_computation.7 | async-start | bytes 589824 | tf_op jit(solution)/shard_map/all_to_all | solution.py:86
  (14 other events, 19.1 us)
Sparse Core Ops, SparseCore 0:
  61.5 69.8 all-gather.6
  133.5 96.3 all-gather.4
where the time goes:
time: 458 us; the launch traced here: 457 us
  waiting for transfers between devices  228 us (50%)
  starting transfers between devices  60.9 us (13%)
  blocking collectives  54.2 us (12%)
  local copies, waits for them, and re-layouts  41.6 us (9%)
  matrix products  40.5 us (9%)
  between operations  15.6 us (3%)
  other arithmetic  15.3 us (3%)
    all_to_all x2, waiting for transfers between devices, sum_at_owner(): lax.all_to_all(tiles, axis, split_axis=0, concat_axis=0, tiled=True)  97.7 us
    all_gather x1, waiting for transfers between devices, local(): latent_weight = lax.all_gather(conv_latent, 'tm', axis=0, tiled=True)  68.7 us
    all_gather x1, blocking collectives, gather_in_order(): tiles = lax.all_gather(tiles, axes[k])  54.2 us
    all_to_all x5, waiting for transfers between devices, copy_for_each(): lax.all_to_all(jnp.broadcast_to(array[None], (devices, *array.shape)), ax...  52.8 us
    all_to_all x5, starting transfers between devices, copy_for_each(): lax.all_to_all(jnp.broadcast_to(array[None], (devices, *array.shape)), ax...  29.7 us
    dot_general x54, matrix products, causal_taps(): jnp.dot(window.reshape(-1, channels_in), kernel, preferred_element_type=j...  20.3 us
    dot_general x27, matrix products, transposed_taps(): lax.dot_general(window.reshape(-1, channels_out), kernel, (((1,), (1,)),...  14 us
    all_to_all x2, starting transfers between devices, sum_at_owner(): lax.all_to_all(tiles, axis, split_axis=0, concat_axis=0, tiled=True)  9.22 us
  transfers between devices with their start and end apart: 17, of which 13 were waited for; matrix products, arithmetic and copies ran while one was open for 12% of the time, Pallas kernels for 0%

commit v1 on v0

--- a/solution.py
+++ b/solution.py
@@ -188,7 +188,10 @@
     mixed = causal_taps(padded, latent_weight, frames_latent, rows_latent, cols_latent)
     refined = (latent_f32 + mixed).astype(jnp.bfloat16)
     band_rows = rows_latent // lax.axis_size("height")
-    own_band = lax.all_to_all(refined, "height", split_axis=1, concat_axis=3, tiled=True)
+    size = lax.axis_size("height")
+    shards = jnp.stack(jnp.split(refined, size, axis=1), axis=0)
+    shards = lax.all_to_all(shards, "height", split_axis=0, concat_axis=0)
+    own_band = jnp.concatenate(shards, axis=3)
     flat_band = own_band.reshape(-1, own_band.shape[-1])
     expanded = jnp.dot(
         flat_band, gather_directly(up_weight, "height", 0), preferred_element_type=jnp.float32

time: 458 us -> 458 us (level)
  no operation moved by 1% of the time
where the time goes in v1:
time: 458 us; the launch traced here: 457 us
  waiting for transfers between devices  228 us (50%)
  starting transfers between devices  61 us (13%)
  blocking collectives  54.2 us (12%)
  local copies, waits for them, and re-layouts  41.6 us (9%)
  matrix products  40.6 us (9%)
  between operations  15.6 us (3%)
  other arithmetic  15.3 us (3%)
    all_to_all x2, waiting for transfers between devices, sum_at_owner(): lax.all_to_all(tiles, axis, split_axis=0, concat_axis=0, tiled=True)  97.6 us
    all_gather x1, waiting for transfers between devices, local(): latent_weight = lax.all_gather(conv_latent, 'tm', axis=0, tiled=True)  68.7 us
    all_gather x1, blocking collectives, gather_in_order(): tiles = lax.all_gather(tiles, axes[k])  54.2 us
    all_to_all x5, waiting for transfers between devices, copy_for_each(): lax.all_to_all(jnp.broadcast_to(array[None], (devices, *array.shape)), ax...  52.8 us
    all_to_all x5, starting transfers between devices, copy_for_each(): lax.all_to_all(jnp.broadcast_to(array[None], (devices, *array.shape)), ax...  29.7 us
    dot_general x54, matrix products, causal_taps(): jnp.dot(window.reshape(-1, channels_in), kernel, preferred_element_type=j...  20.4 us
    dot_general x27, matrix products, transposed_taps(): lax.dot_general(window.reshape(-1, channels_out), kernel, (((1,), (1,)),...  14 us
    all_to_all x2, starting transfers between devices, sum_at_owner(): lax.all_to_all(tiles, axis, split_axis=0, concat_axis=0, tiled=True)  9.23 us
  transfers between devices with their start and end apart: 17, of which 13 were waited for; matrix products, arithmetic and copies ran while one was open for 12% of the time, Pallas kernels for 0%

profile of v1, /device:TPU:2, one launch (start us, length us, event | category | flops | bytes accessed | tf_op | source)
XLA Modules:
  0.0 456.6 jit_solution(9781808321123487798)
XLA Ops:
  7.2 54.2 %all-gather = bf16[1728,256]{1,0:T(8,128)(2,1)} all-gather(bf16[216,256]{1,0:T(8,128)(2,1)} %param.16), channel_id=2, replica_groups=mesh['dp'=16,'tm'=8,'height'=4] {'tm'}, dimensions={0}, use_global_device_ids=true | all-gather | bytes 995328 | tf_op jit(solution)/shard_map/all_gather | solution.py:68
  63.4 10.3 %all-to-all-start = ((f32[8,1,16]{2,1,0:T(1,128)}), f32[8,1,16]{2,1,0:T(1,128)S(1)}, u32[]{:S(2)}, u32[]{:S(2)}) async-start(f32[8,1,16]{2,1,0:T(1,128)} %broadcast_in_dim.10), calls=%async_computation | async-start | bytes 8192 | tf_op jit(solution)/shard_map/all_to_all | solution.py:13
  73.7 0.9 slice.629
  74.6 1.3 collective-permute-start.4
  75.9 8.1 %all-to-all-done = f32[8,1,16]{2,1,0:T(1,128)S(1)} async-done(((f32[8,1,16]{2,1,0:T(1,128)}), f32[8,1,16]{2,1,0:T(1,128)S(1)}, u32[]{:S(2)}, u32[]{:S(2)}) %all-to-all-start) | async-done | bytes 544 | tf_op jit(solution)/shard_map/all_to_all | solution.py:13
  84.4 0.9 fusion.44
  85.3 2.5 collective-permute-start
  87.8 1.0 constant_dynamic-update-slice_fusion.1
  88.8 0.9 collective-permute-done
  89.7 1.0 broadcast_in_dim.11
  90.7 4.5 all-to-all-start.1
  95.2 1.3 collective-permute-start.6
  96.5 4.6 collective-permute-start.5
  101.3 8.3 %all-to-all-done.1 = bf16[4,4,8,16,128]{4,3,2,1,0:T(8,128)(2,1)S(1)} async-done(((bf16[4,4,8,16,128]{4,3,2,1,0:T(8,128)(2,1)}), bf16[4,4,8,16,128]{4,3,2,1,0:T(8,128)(2,1)S(1)}, u32[]{:S(2)}, u32[]{:S(2)}) %all-to-all-start.1) | async-done | bytes 524320 | tf_op jit(solution)/shard_map/all_to_all | solution.py:13
  109.6 1.7 broadcast_in_dim.12
  111.3 3.6 all-to-all-start.3
  115.3 1.4 pad_maximum_fusion.1
  116.7 2.2 fusion.149
  120.0 0.9 copy.59
  121.9 1.2 pad_slice_fusion.1
  123.0 2.4 pad_slice_fusion
  125.4 19.1 %all-to-all-done.3 = bf16[4,128,2048]{1,2,0:T(8,128)(2,1)S(1)} async-done(((bf16[4,128,2048]{1,2,0:T(8,128)(2,1)}), bf16[4,128,2048]{1,2,0:T(8,128)(2,1)S(1)}, u32[]{:S(2)}, u32[]{:S(2)}) %all-to-all-start.3) | async-done | bytes 2097184 | tf_op jit(solution)/shard_map/all_to_all | solution.py:13
  144.5 2.6 copy.63
  147.2 3.9 copy.64
  151.1 2.4 copy.67
  160.1 1.1 convolution_add_fusion.2
  161.2 68.7 %all-gather.5.cloned.1.call-done = bf16[13824,128]{1,0:T(8,128)(2,1)} async-done(((bf16[1728,128]{1,0:T(8,128)(2,1)}), bf16[13824,128]{1,0:T(8,128)(2,1)}) %all-gather.5.cloned.1.call-update) | async-done | bytes 3538960 | tf_op jit(solution)/shard_map/all_gather | solution.py:186
  229.9 1.3 fusion.72
  231.2 1.4 convolution_add_fusion.72
  232.6 1.2 convolution_add_fusion.71
  233.9 1.2 convolution_add_fusion.70
  235.1 1.2 convolution_add_fusion.69
  236.4 1.2 convolution_add_fusion.68
  237.6 1.2 convolution_add_fusion.67
  238.9 1.2 convolution_add_fusion.66
  245.2 4.3 all-to-all-start.2
  249.5 2.2 convolution_add_fusion.1
  251.6 3.6 all-to-all-done.2
  255.2 1.5 copy.61
  256.7 1.5 reshape.490
  258.2 3.8 fusion.146
  266.1 4.8 %all-to-all-start.4 = ((f32[32,1,64]{2,1,0:T(1,128)}), f32[32,1,64]{2,1,0:T(1,128)S(1)}, u32[]{:S(2)}, u32[]{:S(2)}) async-start(f32[32,1,64]{2,1,0:T(1,128)} %broadcast_in_dim.13), calls=%async_computation.4 | async-start | bytes 32768 | tf_op jit(solution)/shard_map/all_to_all | solution.py:13
  271.0 2.0 fusion.74
  273.0 2.2 copy.65
  275.2 2.2 reshape.487
  277.4 5.9 %all-to-all-done.4 = f32[32,1,64]{2,1,0:T(1,128)S(1)} async-done(((f32[32,1,64]{2,1,0:T(1,128)}), f32[32,1,64]{2,1,0:T(1,128)S(1)}, u32[]{:S(2)}, u32[]{:S(2)}) %all-to-all-start.4) | async-done | bytes 8224 | tf_op jit(solution)/shard_map/all_to_all | solution.py:13
  283.8 1.2 slice_multiply_fusion
  287.2 2.8 fusion.145
  290.6 6.5 %all-to-all-start.5 = ((f32[32,1,512]{2,1,0:T(1,128)}), f32[32,1,512]{2,1,0:T(1,128)S(1)}, u32[]{:S(2)}, u32[]{:S(2)}) async-start(f32[32,1,512]{2,1,0:T(1,128)} %broadcast_in_dim.14), calls=%async_computation.5 | async-start | bytes 131072 | tf_op jit(solution)/shard_map/all_to_all | solution.py:13
  297.1 1.4 reshape.486
  298.6 11.5 %all-to-all-done.5 = f32[32,1,512]{2,1,0:T(1,128)S(1)} async-done(((f32[32,1,512]{2,1,0:T(1,128)}), f32[32,1,512]{2,1,0:T(1,128)S(1)}, u32[]{:S(2)}, u32[]{:S(2)}) %all-to-all-start.5) | async-done | bytes 65568 | tf_op jit(solution)/shard_map/all_to_all | solution.py:13
  311.5 2.2 add_convert_fusion
  313.7 2.3 collective-permute-start.1
  316.0 2.5 collective-permute-done.1
  318.5 1.3 collective-permute-start.3
  319.8 4.6 collective-permute-start.2
  325.0 1.5 collective-permute-done.2
  329.5 1.4 copy-done.7
  330.9 5.2 %all-to-all-start.6 = ((f32[8,288,256]{2,1,0:T(8,128)}), f32[8,288,256]{2,1,0:T(8,128)S(1)}, u32[]{:S(2)}, u32[]{:S(2)}) async-start(f32[8,288,256]{2,1,0:T(8,128)} %bitcast.334), calls=%async_computation.6 | async-start | bytes 4718592 | tf_op jit(solution)/shard_map/all_to_all | solution.py:86
  336.2 1.0 pad_maximum_fusion
  337.9 1.3 copy-done.1
  345.8 91.5 %all-to-all-done.6 = f32[8,288,256]{2,1,0:T(8,128)S(1)} async-done(((f32[8,288,256]{2,1,0:T(8,128)}), f32[8,288,256]{2,1,0:T(8,128)S(1)}, u32[]{:S(2)}, u32[]{:S(2)}) %all-to-all-start.6) | async-done | bytes 2359328 | tf_op jit(solution)/shard_map/all_to_all | solution.py:86
  438.2 4.0 all-to-all-start.7
  443.0 6.1 %all-to-all-done.7 = f32[4,72,256]{2,1,0:T(8,128)S(1)} async-done(((f32[4,72,256]{2,1,0:T(8,128)}), f32[4,72,256]{2,1,0:T(8,128)S(1)}, u32[]{:S(2)}, u32[]{:S(2)}) %all-to-all-start.7) | async-done | bytes 294944 | tf_op jit(solution)/shard_map/all_to_all | solution.py:86
  (262 shorter events, 38.0 us)
Async XLA Ops:
  7.2 93.9 %copy-start.51 = (bf16[128,2048]{1,0:T(8,128)(2,1)S(1)}, bf16[128,2048]{1,0:T(8,128)(2,1)}, u32[]{:S(2)}) copy-start(bf16[128,2048]{1,0:T(8,128)(2,1)} %param.13) | copy-start | bytes 1572868
  7.2 143.9 %all-gather.7.cloned.1.call-start = ((), (), s32[]{:S(2)}) async-start(), calls=%async_computation.9 | async-start | bytes 4423680 | tf_op jit(solution)/shard_map/all_gather | solution.py:68
  63.4 20.6 %all-to-all-start = ((f32[8,1,16]{2,1,0:T(1,128)}), f32[8,1,16]{2,1,0:T(1,128)S(1)}, u32[]{:S(2)}, u32[]{:S(2)}) async-start(f32[8,1,16]{2,1,0:T(1,128)} %broadcast_in_dim.10), calls=%async_computation | async-start | bytes 8192 | tf_op jit(solution)/shard_map/all_to_all | solution.py:13
  74.6 20.5 %collective-permute-start.4 = (bf16[2,4,32,256]{3,2,1,0:T(8,128)(2,1)S(1)}, bf16[2,4,32,256]{3,2,1,0:T(8,128)(2,1)S(1)}, u32[]{:S(2)}, u32[]{:S(2)}) collective-permute-start(bf16[2,4,32,256]{3,2,1,0:T(8,128)(2,1)S(1)} %slice.629), channel_id=1, source_target_pairs={{4,0},{8,4},{12,8},{16,12},{20,16},{24,20},{28,24},{5,1},{9,5},{13... | collective-permute-start | bytes 393224 | tf_op jit(solution)/shard_map/ppermute | solution.py:34
  85.3 4.4 collective-permute-start
  90.7 19.0 %all-to-all-start.1 = ((bf16[4,4,8,16,128]{4,3,2,1,0:T(8,128)(2,1)}), bf16[4,4,8,16,128]{4,3,2,1,0:T(8,128)(2,1)S(1)}, u32[]{:S(2)}, u32[]{:S(2)}) async-start(bf16[4,4,8,16,128]{4,3,2,1,0:T(8,128)(2,1)} %broadcast_in_dim.11), calls=%async_computation.1 | async-start | bytes 1048576 | tf_op jit(solution)/shard_map/all_to_all | solution.py:13
  95.1 134.7 %all-gather.5.cloned.1.call-start = ((), (), s32[]{:S(2)}) async-start(), calls=%async_computation.8 | async-start | bytes 3981312 | tf_op jit(solution)/shard_map/all_gather | solution.py:186
  95.2 19.7 %collective-permute-start.6 = (bf16[6,1,32,256]{3,2,1,0:T(8,128)(2,1)S(1)}, bf16[6,1,32,256]{3,2,1,0:T(8,128)(2,1)S(1)}, u32[]{:S(2)}, u32[]{:S(2)}) collective-permute-start(bf16[6,1,32,256]{3,2,1,0:T(8,128)(2,1)S(1)} %get-tuple-element.98), channel_id=1, source_target_pairs={{1,0},{2,1},{3,2},{5,4},{6,5},{7,6},{9,8},{10,9},{11,10},{13,12},{... | collective-permute-start | bytes 294920 | tf_op jit(solution)/shard_map/ppermute | solution.py:58
  96.5 18.4 %collective-permute-start.5 = (bf16[6,1,32,256]{3,2,1,0:T(8,128)(2,1)S(1)}, bf16[6,1,32,256]{3,2,1,0:T(8,128)(2,1)S(1)}, u32[]{:S(2)}, u32[]{:S(2)}) collective-permute-start(bf16[6,1,32,256]{3,2,1,0:T(8,128)(2,1)S(1)} %get-tuple-element.97), channel_id=1, source_target_pairs={{0,1},{1,2},{2,3},{4,5},{5,6},{6,7},{8,9},{9,10},{10,11},{12,13},{... | collective-permute-start | bytes 294920 | tf_op jit(solution)/shard_map/ppermute | solution.py:56
  111.3 33.2 %all-to-all-start.3 = ((bf16[4,128,2048]{1,2,0:T(8,128)(2,1)}), bf16[4,128,2048]{1,2,0:T(8,128)(2,1)S(1)}, u32[]{:S(2)}, u32[]{:S(2)}) async-start(bf16[4,128,2048]{1,2,0:T(8,128)(2,1)} %broadcast_in_dim.12), calls=%async_computation.3 | async-start | bytes 4194304 | tf_op jit(solution)/shard_map/all_to_all | solution.py:13
  151.1 2.5 copy-start.14
  151.1 2.7 copy-start.13
  151.1 3.0 copy-start.12
  151.1 3.3 copy-start.11
  153.5 133.7 %copy-start = (bf16[8,4,216,256]{3,2,1,0:T(8,128)(2,1)}, bf16[8,4,216,256]{3,2,1,0:T(8,128)(2,1)S(1)}, u32[]{:S(2)}) copy-start(bf16[8,4,216,256]{3,2,1,0:T(8,128)(2,1)S(1)} %copy.67) | copy-start | bytes 10616836
  153.5 1.7 copy-start.35
  153.8 1.7 copy-start.10
  154.4 1.4 copy-start.34
  154.7 1.4 copy-start.28
  155.0 1.4 copy-start.33
  155.3 1.4 copy-start.31
  155.5 1.4 copy-start.24
  156.7 1.4 copy-start.27
  157.0 1.4 copy-start.21
  157.3 1.4 copy-start.26
  157.6 1.4 copy-start.25
  229.9 7.8 %copy-start.4 = (bf16[13824,128]{1,0:T(8,128)(2,1)S(1)}, bf16[13824,128]{1,0:T(8,128)(2,1)}, u32[]{:S(2)}) copy-start(bf16[13824,128]{1,0:T(8,128)(2,1)} %all-gather.5.cloned.1.call-done) | copy-start | bytes 10616836
  229.9 10.2 %copy-start.49 = (bf16[2,8,16,512]{3,2,1,0:T(8,128)(2,1)S(1)}, bf16[2,8,16,512]{3,2,1,0:T(8,128)(2,1)}, u32[]{:S(2)}) copy-start(bf16[2,8,16,512]{3,2,1,0:T(8,128)(2,1)} %get-tuple-element.60) | copy-start | bytes 786436
  229.9 10.4 %copy-start.48 = (bf16[2,8,16,512]{3,2,1,0:T(8,128)(2,1)S(1)}, bf16[2,8,16,512]{3,2,1,0:T(8,128)(2,1)}, u32[]{:S(2)}) copy-start(bf16[2,8,16,512]{3,2,1,0:T(8,128)(2,1)} %get-tuple-element.61) | copy-start | bytes 786436
  229.9 10.7 %copy-start.47 = (bf16[2,8,16,512]{3,2,1,0:T(8,128)(2,1)S(1)}, bf16[2,8,16,512]{3,2,1,0:T(8,128)(2,1)}, u32[]{:S(2)}) copy-start(bf16[2,8,16,512]{3,2,1,0:T(8,128)(2,1)} %get-tuple-element.62) | copy-start | bytes 786436
  229.9 10.9 %copy-start.46 = (bf16[2,8,16,512]{3,2,1,0:T(8,128)(2,1)S(1)}, bf16[2,8,16,512]{3,2,1,0:T(8,128)(2,1)}, u32[]{:S(2)}) copy-start(bf16[2,8,16,512]{3,2,1,0:T(8,128)(2,1)} %get-tuple-element.63) | copy-start | bytes 786436
  231.2 9.8 %copy-start.45 = (bf16[2,8,16,512]{3,2,1,0:T(8,128)(2,1)S(1)}, bf16[2,8,16,512]{3,2,1,0:T(8,128)(2,1)}, u32[]{:S(2)}) copy-start(bf16[2,8,16,512]{3,2,1,0:T(8,128)(2,1)} %get-tuple-element.64) | copy-start | bytes 786436
  232.6 8.7 %copy-start.20 = (bf16[2,8,16,4,128]{4,3,2,1,0:T(4,128)(2,1)S(1)}, bf16[2,8,16,4,128]{4,3,2,1,0:T(4,128)(2,1)}, u32[]{:S(2)}) copy-start(bf16[2,8,16,4,128]{4,3,2,1,0:T(4,128)(2,1)} %copy.59) | copy-start | bytes 786436
  233.8 7.7 %copy-start.44 = (bf16[2,8,16,512]{3,2,1,0:T(8,128)(2,1)S(1)}, bf16[2,8,16,512]{3,2,1,0:T(8,128)(2,1)}, u32[]{:S(2)}) copy-start(bf16[2,8,16,512]{3,2,1,0:T(8,128)(2,1)} %get-tuple-element.65) | copy-start | bytes 786436
  235.1 6.6 %copy-start.43 = (bf16[2,8,16,512]{3,2,1,0:T(8,128)(2,1)S(1)}, bf16[2,8,16,512]{3,2,1,0:T(8,128)(2,1)}, u32[]{:S(2)}) copy-start(bf16[2,8,16,512]{3,2,1,0:T(8,128)(2,1)} %get-tuple-element.66) | copy-start | bytes 786436
  236.4 5.6 %copy-start.42 = (bf16[2,8,16,512]{3,2,1,0:T(8,128)(2,1)S(1)}, bf16[2,8,16,512]{3,2,1,0:T(8,128)(2,1)}, u32[]{:S(2)}) copy-start(bf16[2,8,16,512]{3,2,1,0:T(8,128)(2,1)} %get-tuple-element.67) | copy-start | bytes 786436
  237.6 4.6 %copy-start.41 = (bf16[2,8,16,512]{3,2,1,0:T(8,128)(2,1)S(1)}, bf16[2,8,16,512]{3,2,1,0:T(8,128)(2,1)}, u32[]{:S(2)}) copy-start(bf16[2,8,16,512]{3,2,1,0:T(8,128)(2,1)} %get-tuple-element.68) | copy-start | bytes 786436
  238.8 3.6 copy-start.40
  240.1 2.6 copy-start.39
  240.3 2.6 copy-start.38
  240.6 2.6 copy-start.18
  240.8 2.6 copy-start.19
  241.0 2.6 copy-start.17
  241.3 2.6 copy-start.16
  241.5 2.5 copy-start.15
  241.8 2.5 copy-start.37
  242.0 2.5 copy-start.50
  245.2 10.0 %all-to-all-start.2 = ((bf16[4,2,2,16,128]{4,3,2,1,0:T(8,128)(2,1)}), bf16[4,2,2,16,128]{4,3,2,1,0:T(8,128)(2,1)}, u32[]{:S(2)}, u32[]{:S(2)}) async-start(bf16[4,2,2,16,128]{4,3,2,1,0:T(8,128)(2,1)} %pad_maximum_fusion.5), calls=%async_computation.2 | async-start | bytes 131072 | tf_op jit(solution)/shard_map/all_to_all | solution.py:193
  266.1 17.2 %all-to-all-start.4 = ((f32[32,1,64]{2,1,0:T(1,128)}), f32[32,1,64]{2,1,0:T(1,128)S(1)}, u32[]{:S(2)}, u32[]{:S(2)}) async-start(f32[32,1,64]{2,1,0:T(1,128)} %broadcast_in_dim.13), calls=%async_computation.4 | async-start | bytes 32768 | tf_op jit(solution)/shard_map/all_to_all | solution.py:13
  287.2 22.9 %copy-start.55 = (f32[256]{0:T(256)S(1)}, f32[256]{0:T(256)}, u32[]{:S(2)}) copy-start(f32[256]{0:T(256)} %param.14) | copy-start | bytes 3076
  287.2 24.2 %copy-start.56 = (f32[256]{0:T(256)S(1)}, f32[256]{0:T(256)}, u32[]{:S(2)}) copy-start(f32[256]{0:T(256)} %mul.160) | copy-start | bytes 3076
  287.2 24.3 %copy-start.57 = (f32[256]{0:T(256)S(1)}, f32[256]{0:T(256)}, u32[]{:S(2)}) copy-start(f32[256]{0:T(256)} %sub.74) | copy-start | bytes 3076
  287.2 24.3 %copy-start.58 = (f32[256]{0:T(256)S(1)}, f32[256]{0:T(256)}, u32[]{:S(2)}) copy-start(f32[256]{0:T(256)} %param.15) | copy-start | bytes 3076
  290.0 37.0 %copy-start.6 = (bf16[4,4,32,256]{3,2,1,0:T(8,128)(2,1)S(1)}, bf16[4,4,32,256]{3,2,1,0:T(8,128)(2,1)}, u32[]{:S(2)}) copy-start(bf16[4,4,32,256]{3,2,1,0:T(8,128)(2,1)} %param.17) | copy-start | bytes 786436
  290.6 19.4 %all-to-all-start.5 = ((f32[32,1,512]{2,1,0:T(1,128)}), f32[32,1,512]{2,1,0:T(1,128)S(1)}, u32[]{:S(2)}, u32[]{:S(2)}) async-start(f32[32,1,512]{2,1,0:T(1,128)} %broadcast_in_dim.14), calls=%async_computation.5 | async-start | bytes 131072 | tf_op jit(solution)/shard_map/all_to_all | solution.py:13
  298.6 28.9 %copy-start.2 = (f32[4,4,32,256]{3,2,1,0:T(8,128)}, f32[4,4,32,256]{3,2,1,0:T(8,128)S(1)}, u32[]{:S(2)}) copy-start(f32[4,4,32,256]{3,2,1,0:T(8,128)S(1)} %reshape.486) | copy-start | bytes 1572868
  313.7 4.8 %collective-permute-start.1 = (bf16[2,4,32,256]{3,2,1,0:T(8,128)(2,1)S(1)}, bf16[2,4,32,256]{3,2,1,0:T(8,128)(2,1)S(1)}, u32[]{:S(2)}, u32[]{:S(2)}) collective-permute-start(bf16[2,4,32,256]{3,2,1,0:T(8,128)(2,1)S(1)} %slice.690), channel_id=1, source_target_pairs={{0,4},{4,8},{8,12},{12,16},{16,20},{20,24},{24,28},{1,5},{5,9},{9,... | collective-permute-start | bytes 393224 | tf_op jit(solution)/shard_map/ppermute | solution.py:34
  318.5 6.5 %collective-permute-start.3 = (bf16[6,1,32,256]{3,2,1,0:T(8,128)(2,1)S(1)}, bf16[6,1,32,256]{3,2,1,0:T(8,128)(2,1)S(1)}, u32[]{:S(2)}, u32[]{:S(2)}) collective-permute-start(bf16[6,1,32,256]{3,2,1,0:T(8,128)(2,1)S(1)} %get-tuple-element.104), channel_id=1, source_target_pairs={{1,0},{2,1},{3,2},{5,4},{6,5},{7,6},{9,8},{10,9},{11,10},{13,12},{... | collective-permute-start | bytes 294920 | tf_op jit(solution)/shard_map/ppermute | solution.py:58
  319.8 6.8 %collective-permute-start.2 = (bf16[6,1,32,256]{3,2,1,0:T(8,128)(2,1)S(1)}, bf16[6,1,32,256]{3,2,1,0:T(8,128)(2,1)S(1)}, u32[]{:S(2)}, u32[]{:S(2)}) collective-permute-start(bf16[6,1,32,256]{3,2,1,0:T(8,128)(2,1)S(1)} %get-tuple-element.103), channel_id=1, source_target_pairs={{0,1},{1,2},{2,3},{4,5},{5,6},{6,7},{8,9},{9,10},{10,11},{12,13},{... | collective-permute-start | bytes 294920 | tf_op jit(solution)/shard_map/ppermute | solution.py:56
  325.0 3.9 copy-start.53
  330.9 106.5 %all-to-all-start.6 = ((f32[8,288,256]{2,1,0:T(8,128)}), f32[8,288,256]{2,1,0:T(8,128)S(1)}, u32[]{:S(2)}, u32[]{:S(2)}) async-start(f32[8,288,256]{2,1,0:T(8,128)} %bitcast.334), calls=%async_computation.6 | async-start | bytes 4718592 | tf_op jit(solution)/shard_map/all_to_all | solution.py:86
  337.2 2.0 copy-start.1
  345.1 97.1 %copy-start.3 = (f32[4,4,32,256]{3,2,1,0:T(8,128)S(1)}, f32[4,4,32,256]{3,2,1,0:T(8,128)}, u32[]{:S(2)}) copy-start(f32[4,4,32,256]{3,2,1,0:T(8,128)} %copy-done.2) | copy-start | bytes 1572868
  438.2 10.8 %all-to-all-start.7 = ((f32[4,72,256]{2,1,0:T(8,128)}), f32[4,72,256]{2,1,0:T(8,128)S(1)}, u32[]{:S(2)}, u32[]{:S(2)}) async-start(f32[4,72,256]{2,1,0:T(8,128)} %bitcast.337), calls=%async_computation.7 | async-start | bytes 589824 | tf_op jit(solution)/shard_map/all_to_all | solution.py:86
  (12 other events, 16.3 us)
Sparse Core Ops, SparseCore 0:
  61.5 69.8 all-gather.6
  133.5 96.2 all-gather.4
